TPU v7x, 32 devices: a whole 2x2x4 slice. The times are simulated.
32 devices in a mesh: lists: 16 (over z, x, core), sub: 2 (over y).
Axes of the slice: x: 2, y: 2, z: 4, core: 2. Of those that a mesh axis runs over, the one named last changes fastest.
Arguments:
- vectors: bfloat16 [768, 6144], P('sub', 'lists'), may hold values from -6 to 6
- list_ids: int32 [6144], P('lists'), may hold values from 0 to 63
- counts: int32 [16, 16], replicated, may hold values from 0 to 24, as said below
- coarse: bfloat16 [768, 1024], P(None, ('lists', 'sub')), may hold values from -3 to 3
- codebook_init: float32 [768, 256], P('sub'), may hold values from -6 to 6
- codes: int32 [2, 96, 6144], P(None, 'sub', 'lists'), may hold values from 0 to 255
Outputs:
- codebook: float32 [768, 256], P('sub')
- leftover: bfloat16 [768, 6144], P('sub', 'lists')
Inputs may be any that keep to these rules, and one draw needn't show every extreme that they name: `counts`: counts of used slots in each block; in every draw one owner receives full blocks of 24 from every sender. `list_ids`: every slot names one of its block owner's lists.
All inputs are finite; a program needn't handle non-finite values.
Results may differ from a plain program's by a relative error of at most 0.0051.
Values may be sent and summed in bfloat16 or wider, within the bound.
A program may use at most 64 MiB of HBM per device.

v0:
```python
import jax
import jax.numpy as jnp
from jax import lax
from jax.sharding import PartitionSpec as P

K = 256
DS = 8
LISTS_DEV = 64
ITERS = 2


def shards(vectors, list_ids, counts, coarse, codebook_init, codes):
    features, rows = vectors.shape
    owners = lax.axis_size("lists")
    owner = lax.axis_index("lists")
    block = rows // owners
    subspaces = features // DS
    mine = lax.all_to_all(coarse, "sub", split_axis=0, concat_axis=1, tiled=True)
    list_iota = jnp.arange(LISTS_DEV, dtype=jnp.int32)
    arrived = lax.all_to_all(vectors, "lists", split_axis=1, concat_axis=1, tiled=True)
    labels = lax.all_to_all(
        list_ids.reshape(1, rows), "lists", split_axis=1, concat_axis=1, tiled=True
    ).reshape(rows)
    selector = (labels[None, :] == list_iota[:, None]).astype(jnp.bfloat16)
    centre = jnp.dot(mine, selector, preferred_element_type=jnp.float32)
    residual = (arrived.astype(jnp.float32) - centre).astype(jnp.bfloat16)
    block_counts = lax.dynamic_index_in_dim(counts, owner, 1, keepdims=False)
    valid = (jnp.arange(block, dtype=jnp.int32)[None, :] < block_counts[:, None]).reshape(rows)
    code_iota = jnp.arange(K, dtype=jnp.int32)
    split_res = residual.reshape(subspaces, DS, rows)
    group_size = 4
    groups = subspaces // group_size
    grouped_res = split_res.reshape(groups, group_size, DS, rows)
    grouped_codes = jnp.swapaxes(codes, 0, 1).reshape(groups, group_size, ITERS, rows)

    def group_sums(packed):
        sub_res, sub_codes = packed
        one_hot = (sub_codes[:, :, None, :] == code_iota[None, None, :, None]) & valid[
            None, None, None, :
        ]
        one_hot = one_hot.astype(jnp.bfloat16)
        sums = jnp.einsum("gdr,gtkr->tgdk", sub_res, one_hot, preferred_element_type=jnp.float32)
        tally = jnp.swapaxes(jnp.sum(one_hot, axis=3, dtype=jnp.float32), 0, 1)
        return (sums, tally)

    part_sums, part_counts = lax.map(group_sums, (grouped_res, grouped_codes))
    part_sums = jnp.swapaxes(part_sums, 0, 1).reshape(ITERS, features, K)
    part_counts = jnp.swapaxes(part_counts, 0, 1).reshape(ITERS, subspaces, K)
    weight = 0.25 * jnp.sum(counts).astype(jnp.float32) / K
    total_sums, total_counts = lax.psum((part_sums, part_counts), "lists")
    codebook = codebook_init
    for iteration in range(ITERS):
        spread = jnp.repeat(total_counts[iteration], DS, axis=0)
        codebook = (total_sums[iteration] + weight * codebook) / (spread + weight)
    high = codebook.astype(jnp.bfloat16)
    low = (codebook - high.astype(jnp.float32)).astype(jnp.bfloat16)
    books = jnp.concatenate(
        [high.reshape(subspaces, DS, K), low.reshape(subspaces, DS, K)], axis=1
    ).reshape(groups, group_size, 2 * DS, K)

    def group_pick(packed):
        book, sub_codes = packed
        one_hot = (sub_codes[:, None, :] == code_iota[None, :, None]).astype(jnp.bfloat16)
        both = jnp.einsum("gdk,gkr->gdr", book, one_hot, preferred_element_type=jnp.float32)
        return both[:, :DS] + both[:, DS:]

    picked = lax.map(group_pick, (books, grouped_codes[:, :, ITERS - 1]))
    picked = picked.reshape(subspaces, DS, rows)
    leftover = jnp.where(valid[None, None, :], split_res.astype(jnp.float32) - picked, 0.0)
    leftover = leftover.astype(jnp.bfloat16).reshape(features, rows)
    return (codebook, leftover)


def solution(mesh):
    return jax.shard_map(
        shards,
        mesh=mesh,
        in_specs=(
            P("sub", "lists"),
            P("lists"),
            P(),
            P(None, ("lists", "sub")),
            P("sub", None),
            P(None, "sub", "lists"),
        ),
        out_specs=(P("sub", None), P("sub", "lists")),
        check_vma=False,
    )
```

profile of v0, /device:TPU:0, one launch (start us, length us, event | category | flops | bytes accessed | tf_op | source)
XLA Modules:
  0.0 176.7 jit_solution(4619838477152994786)
XLA Ops:
  7.2 1.4 all_to_all.28
  8.6 7.4 %all-to-all-start.1 = ((s32[1,16,24]{2,0,1:T(1,128)}), s32[1,16,24]{2,0,1:T(1,128)S(1)}, u32[]{:S(2)}, u32[]{:S(2)}) async-start(s32[1,16,24]{2,0,1:T(1,128)} %all_to_all.28), calls=%async_computation.1 | async-start | bytes 16384 | tf_op jit(solution)/shard_map/all_to_all | solution.py:21
  16.0 1.9 %copy.21 = bf16[384,384]{0,1:T(8,128)(2,1)} copy(bf16[384,384]{1,0:T(8,128)(2,1)} %param.10) | data formatting | bytes 589824 | tf_op args[0]
  17.8 4.5 %all-to-all-done.1 = s32[1,16,24]{2,0,1:T(1,128)S(1)} async-done(((s32[1,16,24]{2,0,1:T(1,128)}), s32[1,16,24]{2,0,1:T(1,128)S(1)}, u32[]{:S(2)}, u32[]{:S(2)}) %all-to-all-start.1) | async-done | bytes 1568 | tf_op jit(solution)/shard_map/all_to_all | solution.py:21
  22.3 3.5 %all-to-all-start = ((bf16[384,16,24]{0,2,1:T(8,128)(2,1)}), bf16[384,16,24]{0,2,1:T(8,128)(2,1)S(1)}, u32[]{:S(2)}, u32[]{:S(2)}) async-start(bf16[384,16,24]{0,2,1:T(8,128)(2,1)} %bitcast.1), calls=%async_computation | async-start | bytes 589824 | tf_op jit(solution)/shard_map/all_to_all | solution.py:20
  26.6 0.7 reduce_sum.18
  28.6 0.6 reduce.5
  29.4 7.0 %all-to-all-done = bf16[384,16,24]{0,2,1:T(8,128)(2,1)S(1)} async-done(((bf16[384,16,24]{0,2,1:T(8,128)(2,1)}), bf16[384,16,24]{0,2,1:T(8,128)(2,1)S(1)}, u32[]{:S(2)}, u32[]{:S(2)}) %all-to-all-start) | async-done | bytes 294944 | tf_op jit(solution)/shard_map/all_to_all | solution.py:20
  36.4 3.3 %all-to-all-start.2 = ((bf16[2,384,32]{1,2,0:T(8,128)(2,1)}), bf16[2,384,32]{1,2,0:T(8,128)(2,1)S(1)}, u32[]{:S(2)}, u32[]{:S(2)}) async-start(bf16[2,384,32]{1,2,0:T(8,128)(2,1)} %bitcast.93), calls=%async_computation.2 | async-start | bytes 98304 | tf_op jit(solution)/shard_map/all_to_all | solution.py:18
  40.0 3.7 %all-to-all-done.2 = bf16[2,384,32]{1,2,0:T(8,128)(2,1)S(1)} async-done(((bf16[2,384,32]{1,2,0:T(8,128)(2,1)}), bf16[2,384,32]{1,2,0:T(8,128)(2,1)S(1)}, u32[]{:S(2)}, u32[]{:S(2)}) %all-to-all-start.2) | async-done | bytes 49184 | tf_op jit(solution)/shard_map/all_to_all | solution.py:18
  44.0 25.4 %while.24 = (s32[]{:T(128)}, f32[12,2,4,8,256]{4,3,1,2,0:T(8,128)S(1)}, f32[12,2,4,256]{3,1,2,0:T(2,128)}, s32[12,4,2,384]{3,1,0,2:T(4,128)S(1)}, bf16[12,4,8,38...) while((s32[]{:T(128)}, f32[12,2,4,8,256]{4,3,1,2,0:T(8,128)S(1)}, ...), condition=%wide.region_2.3_spmd.clone, body=%wide.region_0.2_spmd.clone.sunk | while | flops 18086272 | bytes 192145 | solution.py:46
  44.2 0.7 fusion.48
  44.9 0.6 convert_reduce_fusion.2
  46.3 0.7 fusion.48
  47.0 0.6 convert_reduce_fusion.2
  48.4 0.7 fusion.48
  50.5 0.7 fusion.48
  52.6 0.7 fusion.48
  53.3 0.6 convert_reduce_fusion.2
  54.8 0.7 fusion.48
  56.9 0.7 fusion.48
  59.0 0.7 fusion.48
  61.1 0.7 fusion.48
  63.2 0.7 fusion.48
  65.3 0.7 fusion.48
  67.4 0.7 fusion.48
  69.4 1.0 copy.25
  70.6 90.5 %all-reduce.3.cloned.1.call-done = (f32[2,384,256]{2,1,0:T(8,128)}, f32[2,48,256]{2,0,1:T(2,128)}) async-done(((f32[2,384,256]{2,1,0:T(8,128)}, f32[2,48,256]{2,0,1:T(2,128)}), (f32[2,384,256]{2,1,0:T(8,128)}, f32[2,48,256]{2,0,1:T(2,128)})) %all-reduce.3.cloned.1.call-update) | async-done | bytes 884752 | tf_op jit(solution)/shard_map/psum | solution.py:50
  161.1 1.1 slice_add_fusion.2
  162.2 2.0 %subtract_convert_fusion = (bf16[384,256]{1,0:T(8,128)(2,1)S(1)}, bf16[384,256]{1,0:T(8,128)(2,1)S(1)}, f32[384,256]{1,0:T(8,128)}) fusion(f32[48,256]{1,0:T(8,128)S(1)} %get-tuple-element.147, f32[48,256]{1,0:T(8,128)S(1)} %get-tuple-element.148, f32[384,256]{1,0:T(8,128)S(1)} %copy-done, f32[2,384,256]{2,1,0:T(8,128)} %get-tuple-element.140, f32[]{:T(128)S(6)} %div.9), kind=kLoop, calls=%fused_computation.43 | loop fusion | flops 983040 | bytes 2064388 | tf_op jit(solution)/shard_map/convert_element_type | solution.py:56
  164.2 4.8 %while.25 = (s32[]{:T(128)}, f32[12,4,8,384]{3,2,1,0:T(8,128)S(1)}, bf16[12,4,16,256]{3,2,1,0:T(8,128)(2,1)S(1)}, s32[12,4,384]{2,1,0:T(4,128)S(1)}, s32[]{:T(128)}) while((s32[]{:T(128)}, f32[12,4,8,384]{3,2,1,0:T(8,128)S(1)}, bf16[12,4,16,256]{3,2,1,0:T(8,128)(2,1)S(1)}, s32[12,4,384]{2,1,0:T(4,128)S(1)}, s32[]{:T(128)}) %tuple.52), condition=%wide.region_7.8_spmd.clone, body=%wide.region_6.7_spmd.clone.sunk | while | flops 12988418 | bytes 297033 | solution.py:67
  169.0 0.8 fusion.31
  (131 shorter events, 22.0 us)
Async XLA Ops:
  7.2 18.7 %copy-start.2 = (bf16[768,32]{0,1:T(8,128)(2,1)S(1)}, bf16[768,32]{0,1:T(8,128)(2,1)}, u32[]{:S(2)}) copy-start(bf16[768,32]{0,1:T(8,128)(2,1)} %param.13) | copy-start | bytes 147460
  7.2 19.3 %copy-start.1 = (s32[2,48,384]{2,1,0:T(8,128)S(1)}, s32[2,48,384]{2,1,0:T(8,128)}, u32[]{:S(2)}) copy-start(s32[2,48,384]{2,1,0:T(8,128)} %param.15) | copy-start | bytes 442372
  8.6 13.7 %all-to-all-start.1 = ((s32[1,16,24]{2,0,1:T(1,128)}), s32[1,16,24]{2,0,1:T(1,128)S(1)}, u32[]{:S(2)}, u32[]{:S(2)}) async-start(s32[1,16,24]{2,0,1:T(1,128)} %all_to_all.28), calls=%async_computation.1 | async-start | bytes 16384 | tf_op jit(solution)/shard_map/all_to_all | solution.py:21
  16.0 10.6 %copy-start.3 = (s32[16,16]{1,0:T(8,128)S(1)}, s32[16,16]{1,0:T(8,128)}, u32[]{:S(2)}) copy-start(s32[16,16]{1,0:T(8,128)} %param.12) | copy-start | bytes 3076
  22.3 14.1 %all-to-all-start = ((bf16[384,16,24]{0,2,1:T(8,128)(2,1)}), bf16[384,16,24]{0,2,1:T(8,128)(2,1)S(1)}, u32[]{:S(2)}, u32[]{:S(2)}) async-start(bf16[384,16,24]{0,2,1:T(8,128)(2,1)} %bitcast.1), calls=%async_computation | async-start | bytes 589824 | tf_op jit(solution)/shard_map/all_to_all | solution.py:20
  36.4 7.3 %all-to-all-start.2 = ((bf16[2,384,32]{1,2,0:T(8,128)(2,1)}), bf16[2,384,32]{1,2,0:T(8,128)(2,1)S(1)}, u32[]{:S(2)}, u32[]{:S(2)}) async-start(bf16[2,384,32]{1,2,0:T(8,128)(2,1)} %bitcast.93), calls=%async_computation.2 | async-start | bytes 98304 | tf_op jit(solution)/shard_map/all_to_all | solution.py:18
  39.7 121.4 %all-reduce.3.cloned.1.call-start = ((), (), s32[]{:S(2)}) async-start(), calls=%async_computation.3 | async-start | bytes 1769472 | tf_op jit(solution)/shard_map/psum | solution.py:50
  70.3 91.8 %copy-start = (f32[384,256]{1,0:T(8,128)S(1)}, f32[384,256]{1,0:T(8,128)}, u32[]{:S(2)}) copy-start(f32[384,256]{1,0:T(8,128)} %param.14) | copy-start | bytes 1179652
Sparse Core Ops, SparseCore 0:
  70.5 90.5 all-reduce.2
where the time goes:
time: 177 us
  waiting for transfers between devices  106 us (60%)
  local copies, waits for them, and re-layouts  14.8 us (8%)
  between operations  14.8 us (8%)
  starting transfers between devices  14.2 us (8%)
  other arithmetic  13.8 us (8%)
  matrix products  12.8 us (7%)
    psum x1, waiting for transfers between devices, shards(): total_sums, total_counts = lax.psum((part_sums, part_counts), 'lists')  90.5 us
    dot_general x12, matrix products, group_sums(): jnp.einsum('gdr,gtkr->tgdk', sub_res, one_hot, preferred_element_type=jnp...  8.24 us
    reduce_sum x12, other arithmetic, group_sums(): tally = jnp.swapaxes(jnp.sum(one_hot, axis=3, dtype=jnp.float32), 0, 1)  7.52 us
    all_to_all x1, starting transfers between devices, shards(): lax.all_to_all(list_ids.reshape(1, rows), 'lists', split_axis=1, concat_a...  7.36 us
    dynamic_update_slice x12, local copies, waits for them, and re-layouts, shards(): part_sums, part_counts = lax.map(group_sums, (grouped_res, grouped_codes))  7.27 us
    all_to_all x1, waiting for transfers between devices, shards(): lax.all_to_all(vectors, 'lists', split_axis=1, concat_axis=1, tiled=True)  7 us
    all_to_all x1, waiting for transfers between devices, shards(): lax.all_to_all(list_ids.reshape(1, rows), 'lists', split_axis=1, concat_a...  4.47 us
    dot_general x12, matrix products, group_pick(): jnp.einsum('gdk,gkr->gdr', book, one_hot, preferred_element_type=jnp.floa...  4.29 us
  transfers between devices with their start and end apart: 4, of which 4 were waited for; matrix products, arithmetic and copies ran while one was open for 3% of the time, Pallas kernels for 0%

commit v1 on v0

--- a/solution.py
+++ b/solution.py
@@ -9,6 +9,18 @@
 ITERS = 2
 
 
+def split_up(array, dim, count):
+    dims = array.shape
+    parts = array.reshape(*dims[:dim], count, dims[dim] // count, *dims[dim + 1 :])
+    return jnp.moveaxis(parts, dim, 0)
+
+
+def in_order(blocks, dim):
+    dims = list(blocks.shape[1:])
+    dims[dim] *= blocks.shape[0]
+    return jnp.moveaxis(blocks, 0, dim).reshape(dims)
+
+
 def shards(vectors, list_ids, counts, coarse, codebook_init, codes):
     features, rows = vectors.shape
     owners = lax.axis_size("lists")
@@ -17,7 +29,14 @@
     subspaces = features // DS
     mine = lax.all_to_all(coarse, "sub", split_axis=0, concat_axis=1, tiled=True)
     list_iota = jnp.arange(LISTS_DEV, dtype=jnp.int32)
-    arrived = lax.all_to_all(vectors, "lists", split_axis=1, concat_axis=1, tiled=True)
+    size, index = (lax.axis_size("lists"), lax.axis_index("lists"))
+    pieces = split_up(vectors, 1, size)
+    gathered = [pieces[index]]
+    for step in range(1, size):
+        sent = pieces[index ^ step]
+        gathered.append(lax.ppermute(sent, "lists", [(i, i ^ step) for i in range(size)]))
+    pieces = jnp.stack(gathered)[index ^ jnp.arange(size)]
+    arrived = in_order(pieces, 1)
     labels = lax.all_to_all(
         list_ids.reshape(1, rows), "lists", split_axis=1, concat_axis=1, tiled=True
     ).reshape(rows)

time: 177 us -> 189 us (1.068)
  starting transfers between devices: 14.2 us -> 31.1 us
  waiting for transfers between devices: 106 us -> 101 us
    ppermute x0 -> x15, starting transfers between devices: none -> 21.8 us  [shards(): lax.ppermute(sent, 'lists', [(i, i ^ step) for i in range(size)])]
    all_to_all x1 -> x0, waiting for transfers between devices: 7 us -> none  [shards(): lax.all_to_all(vectors, 'lists', split_axis=1, concat_axis=1, tiled=True)]
    all_to_all x1, waiting for transfers between devices: 3.66 us -> 0.01 us  [shards(): lax.all_to_all(coarse, 'sub', split_axis=0, concat_axis=1, tiled=True)]
    psum x1, waiting for transfers between devices: 90.5 us -> 94.1 us  [shards(): total_sums, total_counts = lax.psum((part_sums, part_counts), 'lists')]
    all_to_all x1 -> x0, starting transfers between devices: 3.54 us -> none  [shards(): lax.all_to_all(vectors, 'lists', split_axis=1, concat_axis=1, tiled=True)]
    ppermute x0 -> x15, waiting for transfers between devices: none -> 2.8 us  [shards(): lax.ppermute(sent, 'lists', [(i, i ^ step) for i in range(size)])]
  transfers between devices with their start and end apart: 4 -> 18, of which waited for: 4 -> 4; matrix products, arithmetic and copies ran while one was open for 3% -> 2% of each run, Pallas kernels for 0% -> 0%
where the time goes in v1:
time: 189 us
  waiting for transfers between devices  101 us (53%)
  starting transfers between devices  31.1 us (16%)
  between operations  15.1 us (8%)
  local copies, waits for them, and re-layouts  14.3 us (8%)
  other arithmetic  13.7 us (7%)
  matrix products  12.8 us (7%)
    psum x1, waiting for transfers between devices, shards(): total_sums, total_counts = lax.psum((part_sums, part_counts), 'lists')  94.1 us
    ppermute x15, starting transfers between devices, shards(): lax.ppermute(sent, 'lists', [(i, i ^ step) for i in range(size)])  21.8 us
    dot_general x12, matrix products, group_sums(): jnp.einsum('gdr,gtkr->tgdk', sub_res, one_hot, preferred_element_type=jnp...  8.24 us
    reduce_sum x12, other arithmetic, group_sums(): tally = jnp.swapaxes(jnp.sum(one_hot, axis=3, dtype=jnp.float32), 0, 1)  7.52 us
    dynamic_update_slice x12, local copies, waits for them, and re-layouts, shards(): part_sums, part_counts = lax.map(group_sums, (grouped_res, grouped_codes))  7.27 us
    all_to_all x1, starting transfers between devices, shards(): lax.all_to_all(list_ids.reshape(1, rows), 'lists', split_axis=1, concat_a...  6.06 us
    dot_general x12, matrix products, group_pick(): jnp.einsum('gdk,gkr->gdr', book, one_hot, preferred_element_type=jnp.floa...  4.29 us
    all_to_all x1, waiting for transfers between devices, shards(): lax.all_to_all(list_ids.reshape(1, rows), 'lists', split_axis=1, concat_a...  4.14 us
  transfers between devices with their start and end apart: 18, of which 4 were waited for; matrix products, arithmetic and copies ran while one was open for 2% of the time, Pallas kernels for 0%

profile of v1, /device:TPU:0, one launch (start us, length us, event | category | flops | bytes accessed | tf_op | source)
XLA Modules:
  0.0 188.6 jit_solution(4987520160186209619)
XLA Ops:
  7.3 1.2 copy.21
  9.2 2.6 %collective-permute-start.1 = (bf16[384,24]{0,1:T(8,128)(2,1)S(1)}, bf16[384,24]{0,1:T(8,128)(2,1)S(1)}, u32[]{:S(2)}, u32[]{:S(2)}) collective-permute-start(bf16[384,24]{0,1:T(8,128)(2,1)S(1)} %get-tuple-element.158), channel_id=1, source_target_pairs={{0,4},{2,6},{4,0},{6,2},{8,12},{10,14},{12,8},{14,10},{16,20},{18,... | collective-permute-start | bytes 55304 | tf_op jit(solution)/shard_map/ppermute | solution.py:37
  11.8 1.8 collective-permute-start.3
  13.6 0.7 all_to_all.20
  14.3 6.1 %all-to-all-start = ((s32[1,16,24]{2,0,1:T(1,128)}), s32[1,16,24]{2,0,1:T(1,128)S(1)}, u32[]{:S(2)}, u32[]{:S(2)}) async-start(s32[1,16,24]{2,0,1:T(1,128)} %all_to_all.20), calls=%async_computation | async-start | bytes 16384 | tf_op jit(solution)/shard_map/all_to_all | solution.py:40
  22.6 4.1 %all-to-all-done = s32[1,16,24]{2,0,1:T(1,128)S(1)} async-done(((s32[1,16,24]{2,0,1:T(1,128)}), s32[1,16,24]{2,0,1:T(1,128)S(1)}, u32[]{:S(2)}, u32[]{:S(2)}) %all-to-all-start) | async-done | bytes 1568 | tf_op jit(solution)/shard_map/all_to_all | solution.py:40
  26.8 3.3 %all-to-all-start.1 = ((bf16[2,384,32]{1,2,0:T(8,128)(2,1)}), bf16[2,384,32]{1,2,0:T(8,128)(2,1)S(1)}, u32[]{:S(2)}, u32[]{:S(2)}) async-start(bf16[2,384,32]{1,2,0:T(8,128)(2,1)} %bitcast.157), calls=%async_computation.1 | async-start | bytes 98304 | tf_op jit(solution)/shard_map/all_to_all | solution.py:30
  31.9 1.6 collective-permute-start.6
  34.2 2.7 %collective-permute-start.8 = (bf16[384,24]{0,1:T(8,128)(2,1)S(1)}, bf16[384,24]{0,1:T(8,128)(2,1)S(1)}, u32[]{:S(2)}, u32[]{:S(2)}) collective-permute-start(bf16[384,24]{0,1:T(8,128)(2,1)S(1)} %get-tuple-element.151), channel_id=1, source_target_pairs={{0,18},{2,16},{4,22},{6,20},{8,26},{10,24},{12,30},{14,28},{16,2},... | collective-permute-start | bytes 55304 | tf_op jit(solution)/shard_map/ppermute | solution.py:37
  37.5 2.5 %collective-permute-start.10 = (bf16[384,24]{0,1:T(8,128)(2,1)S(1)}, bf16[384,24]{0,1:T(8,128)(2,1)S(1)}, u32[]{:S(2)}, u32[]{:S(2)}) collective-permute-start(bf16[384,24]{0,1:T(8,128)(2,1)S(1)} %get-tuple-element.149), channel_id=1, source_target_pairs={{0,22},{2,20},{4,18},{6,16},{8,30},{10,28},{12,26},{14,24},{16,6},... | collective-permute-start | bytes 55304 | tf_op jit(solution)/shard_map/ppermute | solution.py:37
  40.7 3.6 %collective-permute-start.12 = (bf16[384,24]{0,1:T(8,128)(2,1)S(1)}, bf16[384,24]{0,1:T(8,128)(2,1)S(1)}, u32[]{:S(2)}, u32[]{:S(2)}) collective-permute-start(bf16[384,24]{0,1:T(8,128)(2,1)S(1)} %get-tuple-element.147), channel_id=1, source_target_pairs={{0,26},{2,24},{4,30},{6,28},{8,18},{10,16},{12,22},{14,20},{16,10}... | collective-permute-start | bytes 55304 | tf_op jit(solution)/shard_map/ppermute | solution.py:37
  44.9 3.3 %collective-permute-start.14 = (bf16[384,24]{0,1:T(8,128)(2,1)S(1)}, bf16[384,24]{0,1:T(8,128)(2,1)S(1)}, u32[]{:S(2)}, u32[]{:S(2)}) collective-permute-start(bf16[384,24]{0,1:T(8,128)(2,1)S(1)} %get-tuple-element.145), channel_id=1, source_target_pairs={{0,30},{2,28},{4,26},{6,24},{8,22},{10,20},{12,18},{14,16},{16,14}... | collective-permute-start | bytes 55304 | tf_op jit(solution)/shard_map/ppermute | solution.py:37
  48.3 2.6 %collective-permute-done.13 = bf16[384,24]{0,1:T(8,128)(2,1)S(1)} collective-permute-done((bf16[384,24]{0,1:T(8,128)(2,1)S(1)}, bf16[384,24]{0,1:T(8,128)(2,1)S(1)}, u32[]{:S(2)}, u32[]{:S(2)}) %collective-permute-start.13) | collective-permute-done | bytes 18464 | tf_op jit(solution)/shard_map/ppermute | solution.py:37
  52.3 25.4 %while.24 = (s32[]{:T(128)}, f32[12,2,4,8,256]{4,3,1,2,0:T(8,128)S(1)}, f32[12,2,4,256]{3,1,2,0:T(2,128)}, s32[12,4,2,384]{3,1,0,2:T(4,128)S(1)}, bf16[12,4,8,38...) while((s32[]{:T(128)}, f32[12,2,4,8,256]{4,3,1,2,0:T(8,128)S(1)}, ...), condition=%wide.region_2.3_spmd.clone, body=%wide.region_0.2_spmd.clone.sunk | while | flops 18086272 | bytes 192145 | solution.py:65
  52.5 0.7 fusion.49
  54.6 0.7 fusion.49
  56.7 0.7 fusion.49
  58.8 0.7 fusion.49
  60.9 0.7 fusion.49
  63.0 0.7 fusion.49
  65.2 0.7 fusion.49
  67.3 0.7 fusion.49
  69.4 0.7 fusion.49
  71.5 0.7 fusion.49
  73.6 0.7 fusion.49
  75.7 0.7 fusion.49
  77.6 1.0 copy.25
  78.9 94.1 %all-reduce.3.cloned.1.call-done = (f32[2,384,256]{2,1,0:T(8,128)}, f32[2,48,256]{2,0,1:T(2,128)}) async-done(((f32[2,384,256]{2,1,0:T(8,128)}, f32[2,48,256]{2,0,1:T(2,128)}), (f32[2,384,256]{2,1,0:T(8,128)}, f32[2,48,256]{2,0,1:T(2,128)})) %all-reduce.3.cloned.1.call-update) | async-done | bytes 884752 | tf_op jit(solution)/shard_map/psum | solution.py:69
  173.0 1.1 slice_add_fusion.2
  174.1 2.0 %subtract_convert_fusion = (bf16[384,256]{1,0:T(8,128)(2,1)S(1)}, bf16[384,256]{1,0:T(8,128)(2,1)S(1)}, f32[384,256]{1,0:T(8,128)}) fusion(f32[48,256]{1,0:T(8,128)S(1)} %get-tuple-element.162, f32[48,256]{1,0:T(8,128)S(1)} %get-tuple-element.163, f32[384,256]{1,0:T(8,128)S(1)} %copy-done, f32[2,384,256]{2,1,0:T(8,128)} %get-tuple-element.140, f32[]{:T(128)S(6)} %div.9), kind=kLoop, calls=%fused_computation.44 | loop fusion | flops 983040 | bytes 2064388 | tf_op jit(solution)/shard_map/convert_element_type | solution.py:75
  176.1 4.8 %while.25 = (s32[]{:T(128)}, f32[12,4,8,384]{3,2,1,0:T(8,128)S(1)}, bf16[12,4,16,256]{3,2,1,0:T(8,128)(2,1)S(1)}, s32[12,4,384]{2,1,0:T(4,128)S(1)}, s32[]{:T(128)}) while((s32[]{:T(128)}, f32[12,4,8,384]{3,2,1,0:T(8,128)S(1)}, bf16[12,4,16,256]{3,2,1,0:T(8,128)(2,1)S(1)}, s32[12,4,384]{2,1,0:T(4,128)S(1)}, s32[]{:T(128)}) %tuple.66), condition=%wide.region_7.8_spmd.clone, body=%wide.region_6.7_spmd.clone.sunk | while | flops 12988418 | bytes 297033 | solution.py:86
  180.9 0.8 fusion.31
  (181 shorter events, 29.8 us)
Async XLA Ops:
  7.2 6.5 %copy-start.4 = (s32[384]{0:T(512)S(1)}, s32[384]{0:T(512)}, u32[]{:S(2)}) copy-start(s32[384]{0:T(512)} %param.11) | copy-start | bytes 4612
  7.2 13.3 %copy-start.2 = (bf16[768,32]{0,1:T(8,128)(2,1)S(1)}, bf16[768,32]{0,1:T(8,128)(2,1)}, u32[]{:S(2)}) copy-start(bf16[768,32]{0,1:T(8,128)(2,1)} %param.13) | copy-start | bytes 147460
  7.2 13.9 %copy-start.1 = (s32[2,48,384]{2,1,0:T(8,128)S(1)}, s32[2,48,384]{2,1,0:T(8,128)}, u32[]{:S(2)}) copy-start(s32[2,48,384]{2,1,0:T(8,128)} %param.15) | copy-start | bytes 442372
  7.3 13.9 %copy-start.3 = (s32[16,16]{1,0:T(8,128)S(1)}, s32[16,16]{1,0:T(8,128)}, u32[]{:S(2)}) copy-start(s32[16,16]{1,0:T(8,128)} %param.12) | copy-start | bytes 3076
  8.6 22.7 %collective-permute-start = (bf16[384,24]{0,1:T(8,128)(2,1)S(1)}, bf16[384,24]{0,1:T(8,128)(2,1)S(1)}, u32[]{:S(2)}, u32[]{:S(2)}) collective-permute-start(bf16[384,24]{0,1:T(8,128)(2,1)S(1)} %get-tuple-element.159), channel_id=1, source_target_pairs={{0,2},{2,0},{4,6},{6,4},{8,10},{10,8},{12,14},{14,12},{16,18},{18,... | collective-permute-start | bytes 55304 | tf_op jit(solution)/shard_map/ppermute | solution.py:37
  9.2 22.8 %collective-permute-start.1 = (bf16[384,24]{0,1:T(8,128)(2,1)S(1)}, bf16[384,24]{0,1:T(8,128)(2,1)S(1)}, u32[]{:S(2)}, u32[]{:S(2)}) collective-permute-start(bf16[384,24]{0,1:T(8,128)(2,1)S(1)} %get-tuple-element.158), channel_id=1, source_target_pairs={{0,4},{2,6},{4,0},{6,2},{8,12},{10,14},{12,8},{14,10},{16,20},{18,... | collective-permute-start | bytes 55304 | tf_op jit(solution)/shard_map/ppermute | solution.py:37
  11.7 21.8 %collective-permute-start.2 = (bf16[384,24]{0,1:T(8,128)(2,1)S(1)}, bf16[384,24]{0,1:T(8,128)(2,1)S(1)}, u32[]{:S(2)}, u32[]{:S(2)}) collective-permute-start(bf16[384,24]{0,1:T(8,128)(2,1)S(1)} %get-tuple-element.157), channel_id=1, source_target_pairs={{0,6},{2,4},{4,2},{6,0},{8,14},{10,12},{12,10},{14,8},{16,22},{18,... | collective-permute-start | bytes 55304 | tf_op jit(solution)/shard_map/ppermute | solution.py:37
  11.8 22.4 %collective-permute-start.3 = (bf16[384,24]{0,1:T(8,128)(2,1)S(1)}, bf16[384,24]{0,1:T(8,128)(2,1)S(1)}, u32[]{:S(2)}, u32[]{:S(2)}) collective-permute-start(bf16[384,24]{0,1:T(8,128)(2,1)S(1)} %get-tuple-element.156), channel_id=1, source_target_pairs={{0,8},{2,10},{4,12},{6,14},{8,0},{10,2},{12,4},{14,6},{16,24},{18,... | collective-permute-start | bytes 55304 | tf_op jit(solution)/shard_map/ppermute | solution.py:37
  13.6 23.3 %collective-permute-start.4 = (bf16[384,24]{0,1:T(8,128)(2,1)S(1)}, bf16[384,24]{0,1:T(8,128)(2,1)S(1)}, u32[]{:S(2)}, u32[]{:S(2)}) collective-permute-start(bf16[384,24]{0,1:T(8,128)(2,1)S(1)} %get-tuple-element.155), channel_id=1, source_target_pairs={{0,10},{2,8},{4,14},{6,12},{8,2},{10,0},{12,6},{14,4},{16,26},{18,... | collective-permute-start | bytes 55304 | tf_op jit(solution)/shard_map/ppermute | solution.py:37
  14.3 12.5 %all-to-all-start = ((s32[1,16,24]{2,0,1:T(1,128)}), s32[1,16,24]{2,0,1:T(1,128)S(1)}, u32[]{:S(2)}, u32[]{:S(2)}) async-start(s32[1,16,24]{2,0,1:T(1,128)} %all_to_all.20), calls=%async_computation | async-start | bytes 16384 | tf_op jit(solution)/shard_map/all_to_all | solution.py:40
  26.8 25.2 %all-to-all-start.1 = ((bf16[2,384,32]{1,2,0:T(8,128)(2,1)}), bf16[2,384,32]{1,2,0:T(8,128)(2,1)S(1)}, u32[]{:S(2)}, u32[]{:S(2)}) async-start(bf16[2,384,32]{1,2,0:T(8,128)(2,1)} %bitcast.157), calls=%async_computation.1 | async-start | bytes 98304 | tf_op jit(solution)/shard_map/all_to_all | solution.py:30
  30.1 142.9 %all-reduce.3.cloned.1.call-start = ((), (), s32[]{:S(2)}) async-start(), calls=%async_computation.2 | async-start | bytes 1769472 | tf_op jit(solution)/shard_map/psum | solution.py:69
  31.3 6.2 %collective-permute-start.5 = (bf16[384,24]{0,1:T(8,128)(2,1)S(1)}, bf16[384,24]{0,1:T(8,128)(2,1)S(1)}, u32[]{:S(2)}, u32[]{:S(2)}) collective-permute-start(bf16[384,24]{0,1:T(8,128)(2,1)S(1)} %get-tuple-element.154), channel_id=1, source_target_pairs={{0,12},{2,14},{4,8},{6,10},{8,4},{10,6},{12,0},{14,2},{16,28},{18,... | collective-permute-start | bytes 55304 | tf_op jit(solution)/shard_map/ppermute | solution.py:37
  31.9 8.0 %collective-permute-start.6 = (bf16[384,24]{0,1:T(8,128)(2,1)S(1)}, bf16[384,24]{0,1:T(8,128)(2,1)S(1)}, u32[]{:S(2)}, u32[]{:S(2)}) collective-permute-start(bf16[384,24]{0,1:T(8,128)(2,1)S(1)} %get-tuple-element.153), channel_id=1, source_target_pairs={{0,14},{2,12},{4,10},{6,8},{8,6},{10,4},{12,2},{14,0},{16,30},{18,... | collective-permute-start | bytes 55304 | tf_op jit(solution)/shard_map/ppermute | solution.py:37
  33.5 7.2 %collective-permute-start.7 = (bf16[384,24]{0,1:T(8,128)(2,1)S(1)}, bf16[384,24]{0,1:T(8,128)(2,1)S(1)}, u32[]{:S(2)}, u32[]{:S(2)}) collective-permute-start(bf16[384,24]{0,1:T(8,128)(2,1)S(1)} %get-tuple-element.152), channel_id=1, source_target_pairs={{0,16},{2,18},{4,20},{6,22},{8,24},{10,26},{12,28},{14,30},{16,0},... | collective-permute-start | bytes 55304 | tf_op jit(solution)/shard_map/ppermute | solution.py:37
  34.2 10.1 %collective-permute-start.8 = (bf16[384,24]{0,1:T(8,128)(2,1)S(1)}, bf16[384,24]{0,1:T(8,128)(2,1)S(1)}, u32[]{:S(2)}, u32[]{:S(2)}) collective-permute-start(bf16[384,24]{0,1:T(8,128)(2,1)S(1)} %get-tuple-element.151), channel_id=1, source_target_pairs={{0,18},{2,16},{4,22},{6,20},{8,26},{10,24},{12,30},{14,28},{16,2},... | collective-permute-start | bytes 55304 | tf_op jit(solution)/shard_map/ppermute | solution.py:37
  36.9 8.0 %collective-permute-start.9 = (bf16[384,24]{0,1:T(8,128)(2,1)S(1)}, bf16[384,24]{0,1:T(8,128)(2,1)S(1)}, u32[]{:S(2)}, u32[]{:S(2)}) collective-permute-start(bf16[384,24]{0,1:T(8,128)(2,1)S(1)} %get-tuple-element.150), channel_id=1, source_target_pairs={{0,20},{2,22},{4,16},{6,18},{8,28},{10,30},{12,24},{14,26},{16,4},... | collective-permute-start | bytes 55304 | tf_op jit(solution)/shard_map/ppermute | solution.py:37
  37.5 10.7 %collective-permute-start.10 = (bf16[384,24]{0,1:T(8,128)(2,1)S(1)}, bf16[384,24]{0,1:T(8,128)(2,1)S(1)}, u32[]{:S(2)}, u32[]{:S(2)}) collective-permute-start(bf16[384,24]{0,1:T(8,128)(2,1)S(1)} %get-tuple-element.149), channel_id=1, source_target_pairs={{0,22},{2,20},{4,18},{6,16},{8,30},{10,28},{12,26},{14,24},{16,6},... | collective-permute-start | bytes 55304 | tf_op jit(solution)/shard_map/ppermute | solution.py:37
  40.0 8.3 %collective-permute-start.11 = (bf16[384,24]{0,1:T(8,128)(2,1)S(1)}, bf16[384,24]{0,1:T(8,128)(2,1)S(1)}, u32[]{:S(2)}, u32[]{:S(2)}) collective-permute-start(bf16[384,24]{0,1:T(8,128)(2,1)S(1)} %get-tuple-element.148), channel_id=1, source_target_pairs={{0,24},{2,26},{4,28},{6,30},{8,16},{10,18},{12,20},{14,22},{16,8},... | collective-permute-start | bytes 55304 | tf_op jit(solution)/shard_map/ppermute | solution.py:37
  40.7 7.6 %collective-permute-start.12 = (bf16[384,24]{0,1:T(8,128)(2,1)S(1)}, bf16[384,24]{0,1:T(8,128)(2,1)S(1)}, u32[]{:S(2)}, u32[]{:S(2)}) collective-permute-start(bf16[384,24]{0,1:T(8,128)(2,1)S(1)} %get-tuple-element.147), channel_id=1, source_target_pairs={{0,26},{2,24},{4,30},{6,28},{8,18},{10,16},{12,22},{14,20},{16,10}... | collective-permute-start | bytes 55304 | tf_op jit(solution)/shard_map/ppermute | solution.py:37
  44.3 6.6 %collective-permute-start.13 = (bf16[384,24]{0,1:T(8,128)(2,1)S(1)}, bf16[384,24]{0,1:T(8,128)(2,1)S(1)}, u32[]{:S(2)}, u32[]{:S(2)}) collective-permute-start(bf16[384,24]{0,1:T(8,128)(2,1)S(1)} %get-tuple-element.146), channel_id=1, source_target_pairs={{0,28},{2,30},{4,24},{6,26},{8,20},{10,22},{12,16},{14,18},{16,12}... | collective-permute-start | bytes 55304 | tf_op jit(solution)/shard_map/ppermute | solution.py:37
  44.9 6.1 %collective-permute-start.14 = (bf16[384,24]{0,1:T(8,128)(2,1)S(1)}, bf16[384,24]{0,1:T(8,128)(2,1)S(1)}, u32[]{:S(2)}, u32[]{:S(2)}) collective-permute-start(bf16[384,24]{0,1:T(8,128)(2,1)S(1)} %get-tuple-element.145), channel_id=1, source_target_pairs={{0,30},{2,28},{4,26},{6,24},{8,22},{10,20},{12,18},{14,16},{16,14}... | collective-permute-start | bytes 55304 | tf_op jit(solution)/shard_map/ppermute | solution.py:37
  78.7 95.4 %copy-start = (f32[384,256]{1,0:T(8,128)S(1)}, f32[384,256]{1,0:T(8,128)}, u32[]{:S(2)}) copy-start(f32[384,256]{1,0:T(8,128)} %param.14) | copy-start | bytes 1179652
Sparse Core Ops, SparseCore 0:
  78.8 94.1 all-reduce.2
